TPU v7x, 32 devices: a whole 2x2x4 slice. The times are simulated.
32 devices in a mesh: lr: 8 (over y, x, core), lc: 4 (over z).
Axes of the slice: x: 2, y: 2, z: 4, core: 2. Of those that a mesh axis runs over, the one named last changes fastest.
Arguments:
- queries: bfloat16 [2048, 768], P(('lr', 'lc')), may hold values from -6 to 6
- probes: int32 [2048, 16], P(('lr', 'lc')), may hold values from 0 to 255, as said below
- assign: int32 [2048], P(('lr', 'lc')), may hold values from 0 to 255, as said below
- list_rows: bfloat16 [256, 1024, 768], P(('lr', 'lc')), may hold values from -0.21875 to 0.21875
- list_fill: int32 [256], P(('lr', 'lc')), may hold values from 1 to 1024
- centroids: float32 [256, 768], P(('lr', 'lc')), may hold values from -6 to 6
- list_sums: float32 [256, 768], P(('lr', 'lc')), may hold values from -6 to 6
Outputs:
- dup_max: float32 [2048, 16], P(('lr', 'lc'))
- codes: bfloat16 [256, 16, 768], P(('lr', 'lc'))
- scales: float32 [256, 16], P(('lr', 'lc'))
- new_sums: float32 [256, 768], P(('lr', 'lc'))
Inputs may be any that keep to these rules, and one draw needn't show every extreme that they name: A list id is 8 times its owner's device index along lr+lc plus its place there. The probe pairs of one device's new vectors name lists of one owner at most 64 times, and one list is named by at most 256 pairs over all new vectors; both bounds are reached. A vector's probes may repeat a list. `assign`: one device's new vectors go to lists of one owner at most 4 times, and one list receives at most 16 new vectors; both bounds are reached.
All inputs are finite; a program needn't handle non-finite values. Where the computation divides by a largest or mean magnitude, that divisor is 1e-20 or more.
Results may differ from a plain program's by a relative error of at most 0.001.
Values may be sent and summed in bfloat16 or wider, within the bound.
No kernel may reach another device: no remote copies, remote signals or barrier semaphores. Data moves between devices by JAX's collectives and lax.ppermute only.
A program may use at most 64 MiB of HBM per device.

v0:
```python
import jax
import jax.numpy as jnp
from jax import lax
from jax.sharding import PartitionSpec as P


def select_rows(index, count, table):
    onehot = (index[:, None] == jnp.arange(count, dtype=jnp.int32)[None, :]).astype(table.dtype)
    if table.dtype == jnp.bfloat16:
        return jnp.dot(onehot, table, preferred_element_type=jnp.float32).astype(jnp.bfloat16)
    return jnp.dot(
        onehot, table, precision=lax.Precision.HIGHEST, preferred_element_type=jnp.float32
    )


def route(list_ids, group_size, capacity, list_count):
    owners = list_ids // list_count
    local_ids = list_ids % list_count
    matches = (owners[:, None] == jnp.arange(group_size, dtype=jnp.int32)[None, :]).astype(
        jnp.int32
    )
    order_in = jnp.sum(jnp.cumsum(matches, axis=0) * matches, axis=1) - 1
    placed = owners * capacity + order_in
    slot_ids = jnp.arange(group_size * capacity, dtype=jnp.int32)
    hit = placed[None, :] == slot_ids[:, None]
    filled = jnp.any(hit, axis=1)
    item_ids = jnp.arange(list_ids.shape[0], dtype=jnp.int32)
    source = jnp.where(filled, jnp.sum(jnp.where(hit, item_ids[None, :], 0), axis=1), -1)
    target_list = jnp.where(filled, jnp.sum(jnp.where(hit, local_ids[None, :], 0), axis=1), -1)
    return (placed, source, target_list)


def rank_in_list(flat_lists, list_count):
    matches = (flat_lists[:, None] == jnp.arange(list_count, dtype=jnp.int32)[None, :]).astype(
        jnp.int32
    )
    return (matches, jnp.sum(jnp.cumsum(matches, axis=0) * matches, axis=1) - 1)


def grouped_scores(flat_vectors, flat_lists, list_rows, list_fill, per_list):
    list_count = list_rows.shape[0]
    row_count = list_rows.shape[1]
    bucket_count = list_count * per_list
    matches, order_in = rank_in_list(flat_lists, list_count)
    bucket = jnp.where(flat_lists >= 0, flat_lists * per_list + order_in, bucket_count)
    selector = jnp.arange(bucket_count, dtype=jnp.int32)[:, None] == bucket[None, :]
    grouped = jnp.dot(
        selector.astype(jnp.bfloat16), flat_vectors, preferred_element_type=jnp.float32
    ).astype(jnp.bfloat16)
    grouped = grouped.reshape(list_count, per_list, flat_vectors.shape[1])
    scores = jnp.einsum("lkd,lrd->lkr", grouped, list_rows, preferred_element_type=jnp.float32)
    scores = jnp.where(
        jnp.arange(row_count, dtype=jnp.int32)[None, None, :] < list_fill[:, None, None],
        scores,
        -jnp.inf,
    )
    best_flat = jnp.max(scores, axis=2).reshape(-1)
    return lax.dot_general(
        selector.astype(jnp.float32),
        best_flat,
        (((0,), (0,)), ((), ())),
        precision=lax.Precision.HIGHEST,
        preferred_element_type=jnp.float32,
    )


def local(queries, probes, assign, list_rows, list_fill, centroids, list_sums):
    grid_rows = lax.axis_size("lr")
    grid_cols = lax.axis_size("lc")
    group_size = grid_rows * grid_cols
    list_count = list_rows.shape[0]
    query_count = queries.shape[0]
    probe_count = probes.shape[1]
    feature_dim = queries.shape[1]
    pair_cap = 2 * query_count * probe_count // group_size
    append_cap = max(2, 2 * query_count // group_size)
    per_list = group_size * pair_cap // list_count
    append_slots = group_size * append_cap // list_count
    placed, source, target_list = route(probes.reshape(-1), group_size, pair_cap, list_count)
    source_query = jnp.where(source >= 0, source // probe_count, -1)
    sent_vectors = select_rows(source_query, query_count, queries).reshape(
        group_size, pair_cap, feature_dim
    )
    sent_lists = target_list.reshape(group_size, pair_cap)
    vectors = lax.all_to_all(sent_vectors, ("lr", "lc"), split_axis=0, concat_axis=0, tiled=True)
    lists = lax.all_to_all(sent_lists, ("lr", "lc"), split_axis=0, concat_axis=0, tiled=True)
    flat_vectors = vectors.reshape(-1, feature_dim)
    flat_lists = lists.reshape(-1)
    best = grouped_scores(flat_vectors, flat_lists, list_rows, list_fill, per_list)
    maxima = lax.all_to_all(
        best.reshape(lists.shape), ("lr", "lc"), split_axis=0, concat_axis=0, tiled=True
    )
    dup_max = select_rows(placed, group_size * pair_cap, maxima.reshape(-1, 1)).reshape(
        query_count, probe_count
    )
    append_placed, append_source, append_target = route(assign, group_size, append_cap, list_count)
    new_vectors = select_rows(append_source, query_count, queries).reshape(
        group_size, append_cap, feature_dim
    )
    new_lists = append_target.reshape(group_size, append_cap)
    got_new, got_ids = (
        lax.all_to_all(new_vectors, ("lr", "lc"), split_axis=0, concat_axis=0, tiled=True),
        lax.all_to_all(new_lists, ("lr", "lc"), split_axis=0, concat_axis=0, tiled=True),
    )
    flat_new = got_new.reshape(-1, feature_dim)
    flat_ids = got_ids.reshape(-1)
    matches, order_in = rank_in_list(flat_ids, list_count)
    weights = matches.astype(jnp.float32)
    center = jnp.dot(
        weights, centroids, precision=lax.Precision.HIGHEST, preferred_element_type=jnp.float32
    )
    residual = flat_new.astype(jnp.float32) - center
    row_scale = jnp.max(jnp.abs(residual), axis=1) + 1e-06
    code_rows = (residual / row_scale[:, None]).astype(jnp.bfloat16)
    slot_count = list_count * append_slots
    slot_at = jnp.where(flat_ids >= 0, flat_ids * append_slots + order_in, slot_count)
    placement = jnp.arange(slot_count, dtype=jnp.int32)[:, None] == slot_at[None, :]
    codes = jnp.dot(
        placement.astype(jnp.bfloat16), code_rows, preferred_element_type=jnp.float32
    ).astype(jnp.bfloat16)
    scales = jnp.dot(
        placement.astype(jnp.float32),
        row_scale,
        precision=lax.Precision.HIGHEST,
        preferred_element_type=jnp.float32,
    )
    added = lax.dot_general(
        weights,
        residual,
        (((0,), (0,)), ((), ())),
        precision=lax.Precision.HIGHEST,
        preferred_element_type=jnp.float32,
    )
    new_sums = list_sums + added
    return (
        dup_max,
        codes.reshape(list_count, append_slots, feature_dim),
        scales.reshape(list_count, append_slots),
        new_sums,
    )


def solution(mesh):
    return jax.shard_map(
        local,
        mesh=mesh,
        in_specs=(
            P(("lr", "lc"), None),
            P(("lr", "lc"), None),
            P(("lr", "lc")),
            P(("lr", "lc"), None, None),
            P(("lr", "lc")),
            P(("lr", "lc"), None),
            P(("lr", "lc"), None),
        ),
        out_specs=(
            P(("lr", "lc"), None),
            P(("lr", "lc"), None, None),
            P(("lr", "lc"), None),
            P(("lr", "lc"), None),
        ),
        check_vma=False,
    )
```

profile of v0, /device:TPU:0, one launch (start us, length us, event | category | flops | bytes accessed | tf_op | source)
XLA Modules:
  0.0 181.3 jit_solution(6461436222097683330)
XLA Ops:
  0.6 0.7 and_select_fusion
  1.9 0.7 select_n.152
  2.6 7.3 %all-to-all-start.3 = ((s32[32,1,4]{2,1,0:T(1,128)}), s32[32,1,4]{2,1,0:T(1,128)S(1)}, u32[]{:S(2)}, u32[]{:S(2)}) async-start(s32[32,1,4]{2,1,0:T(1,128)} %bitcast.12), calls=%async_computation.3 | async-start | bytes 32768 | tf_op jit(solution)/shard_map/all_to_all | solution.py:103
  9.9 0.8 copy.29
  10.9 9.0 %reduce-window.14 = s32[32,8,128]{2,1,0:T(8,128)S(1)} reduce-window(s32[32,8,128]{2,1,0:T(8,128)S(1)} %fusion.11, s32[]{:T(128)} %constant.88.clone.1), window={size=1x1x128 pad=0_0x0_0x127_0}, to_apply=%region_0.1 | reduce-window | flops 4161536 | bytes 262148 | tf_op jit(solution)/shard_map/reduce-window
  20.5 1.0 fusion.2
  21.5 2.7 %select_reduce_fusion.1 = (s32[2048]{0:T(1024)S(1)}, s32[2048]{0:T(1024)S(1)}) fusion(s32[1024]{0:T(1024)S(1)} %get-tuple-element.9, s32[1024]{0:T(1024)S(1)} %get-tuple-element.10), kind=kLoop, calls=%fused_computation.4 | loop fusion | flops 10481664 | bytes 24576 | tf_op jit(solution)/shard_map/reduce_sum | solution.py:28
  24.2 0.7 select_n.141
  24.9 5.8 %all-to-all-start = ((s32[32,1,64]{2,1,0:T(1,128)}), s32[32,1,64]{2,1,0:T(1,128)S(1)}, u32[]{:S(2)}, u32[]{:S(2)}) async-start(s32[32,1,64]{2,1,0:T(1,128)} %select_n.141), calls=%async_computation | async-start | bytes 32768 | tf_op jit(solution)/shard_map/all_to_all | solution.py:86
  31.0 0.7 reshape.381
  31.7 6.1 %all-to-all-done = s32[32,1,64]{2,1,0:T(1,128)S(1)} async-done(((s32[32,1,64]{2,1,0:T(1,128)}), s32[32,1,64]{2,1,0:T(1,128)S(1)}, u32[]{:S(2)}, u32[]{:S(2)}) %all-to-all-start) | async-done | bytes 8224 | tf_op jit(solution)/shard_map/all_to_all | solution.py:86
  37.8 2.6 %all-to-all-start.4 = ((bf16[32,4,768]{2,1,0:T(4,128)(2,1)}), bf16[32,4,768]{2,1,0:T(4,128)(2,1)S(1)}, u32[]{:S(2)}, u32[]{:S(2)}) async-start(bf16[32,4,768]{2,1,0:T(4,128)(2,1)} %reshape.381), calls=%async_computation.4 | async-start | bytes 393216 | tf_op jit(solution)/shard_map/all_to_all | solution.py:102
  40.4 2.5 %convolution_convert_fusion = bf16[2048,768]{1,0:T(8,128)(2,1)} fusion(bf16[64,768]{1,0:T(8,128)(2,1)S(1)} %copy-done, s32[2048]{0:T(1024)S(1)} %get-tuple-element.11), kind=kOutput, calls=%fused_computation.13 | convolution fusion | flops 203030528 | bytes 3252224 | tf_op jit(solution)/shard_map/dot_general | solution.py:10
  42.9 6.9 %all-to-all-done.4 = bf16[32,4,768]{2,1,0:T(4,128)(2,1)S(1)} async-done(((bf16[32,4,768]{2,1,0:T(4,128)(2,1)}), bf16[32,4,768]{2,1,0:T(4,128)(2,1)S(1)}, u32[]{:S(2)}, u32[]{:S(2)}) %all-to-all-start.4) | async-done | bytes 196640 | tf_op jit(solution)/shard_map/all_to_all | solution.py:102
  49.7 3.0 %all-to-all-start.1 = ((bf16[32,64,768]{2,1,0:T(8,128)(2,1)}), bf16[32,64,768]{2,1,0:T(8,128)(2,1)S(1)}, u32[]{:S(2)}, u32[]{:S(2)}) async-start(bf16[32,64,768]{2,1,0:T(8,128)(2,1)} %bitcast.5), calls=%async_computation.1 | async-start | bytes 6291456 | tf_op jit(solution)/shard_map/all_to_all | solution.py:85
  55.4 0.7 fusion.16
  56.1 1.0 reduce_window_sum.57
  58.6 4.2 %reduce-window.16 = s32[8,16,128]{2,1,0:T(8,128)S(1)} reduce-window(s32[8,16,128]{2,1,0:T(8,128)} %fusion.17, s32[]{:T(128)} %constant.88.clone.1), window={size=1x1x128 pad=0_0x0_0x127_0}, to_apply=%region_5.6 | reduce-window | flops 2080768 | bytes 131076 | tf_op jit(solution)/shard_map/reduce-window.2
  63.2 0.7 reduce.13
  64.2 4.6 %iota_compare_fusion.1 = pred[2048,2048]{1,0:T(32,128)(4,1)} fusion(s32[2048]{0:T(1024)S(1)} %add_select_fusion.2), kind=kLoop, calls=%fused_computation.1 | loop fusion | flops 4194304 | bytes 4202496 | tf_op jit(solution)/shard_map/eq | solution.py:46
  68.7 0.8 reshape.384
  69.5 1.6 abs_reduce_fusion
  71.1 1.0 convolution_add_fusion
  72.2 1.0 convolution_convert_fusion.2
  73.1 49.6 %all-to-all-done.1 = bf16[32,64,768]{2,1,0:T(8,128)(2,1)S(1)} async-done(((bf16[32,64,768]{2,1,0:T(8,128)(2,1)}), bf16[32,64,768]{2,1,0:T(8,128)(2,1)S(1)}, u32[]{:S(2)}, u32[]{:S(2)}) %all-to-all-start.1) | async-done | bytes 3145760 | tf_op jit(solution)/shard_map/all_to_all | solution.py:85
  122.7 8.6 %fusion.7 = bf16[2048,768]{1,0:T(8,128)(2,1)} fusion(bf16[2048,768]{1,0:T(8,128)(2,1)S(1)} %bitcast.60, s32[2048]{0:T(1024)S(1)} %add_select_fusion.2), kind=kOutput, calls=%fused_computation.14 | convolution fusion | flops 6448218112 | bytes 6299648 | tf_op jit(solution)/shard_map/dot_general | solution.py:47
  131.3 9.1 %select_reduce_fusion = f32[8,256]{1,0:T(8,128)S(1)} fusion(pred[8,1024]{1,0:T(8,128)(4,1)S(1)} %copy-done.6, bf16[8,256,768]{2,1,0:T(8,128)(2,1)} %bitcast.66, bf16[8,1024,768]{2,1,0:T(8,128)(2,1)} %param.10), kind=kOutput, calls=%fused_computation.3 | convolution fusion | flops 3225417728 | bytes 15745024 | tf_op jit(solution)/shard_map/lkd,lrd->lkr/dot_general | solution.py:51
  140.4 12.1 %convolution_bitcast_fusion = f32[32,1,64]{2,1,0:T(1,128)} fusion(pred[32,64,2048]{2,1,0:T(32,128)(4,1)} %bitcast.59, f32[2048,1,1]{0,1,2:T(1,128)S(1)} %reshape.385), kind=kOutput, calls=%fused_computation.19 | convolution fusion | flops 50331648 | bytes 4210688 | tf_op jit(solution)/shard_map/dot_general | solution.py:58
  152.6 5.1 %all-to-all-start.2 = ((f32[32,1,64]{2,1,0:T(1,128)}), f32[32,1,64]{2,1,0:T(1,128)S(1)}, u32[]{:S(2)}, u32[]{:S(2)}) async-start(f32[32,1,64]{2,1,0:T(1,128)} %convolution_bitcast_fusion), calls=%async_computation.2 | async-start | bytes 32768 | tf_op jit(solution)/shard_map/all_to_all | solution.py:90
  157.8 0.7 reshape.383
  158.5 6.1 %all-to-all-done.2 = f32[32,1,64]{2,1,0:T(1,128)S(1)} async-done(((f32[32,1,64]{2,1,0:T(1,128)}), f32[32,1,64]{2,1,0:T(1,128)S(1)}, u32[]{:S(2)}, u32[]{:S(2)}) %all-to-all-start.2) | async-done | bytes 8224 | tf_op jit(solution)/shard_map/all_to_all | solution.py:90
  165.9 14.7 %fusion.4 = f32[1,64,16]{2,0,1:T(1,128)S(1)} fusion(f32[2048,1,1]{0,1,2:T(1,128)S(1)} %reshape.387, s32[64,16]{1,0:T(8,128)S(1)} %copy-done.1), kind=kOutput, calls=%fused_computation.11 | convolution fusion | flops 27262976 | bytes 16384 | tf_op jit(solution)/shard_map/dot_general | solution.py:11
  (64 shorter events, 8.4 us)
Async XLA Ops:
  0.6 30.1 %copy-start = (bf16[64,768]{1,0:T(8,128)(2,1)S(1)}, bf16[64,768]{1,0:T(8,128)(2,1)}, u32[]{:S(2)}) copy-start(bf16[64,768]{1,0:T(8,128)(2,1)} %param.7) | copy-start | bytes 294916
  2.6 22.2 %all-to-all-start.3 = ((s32[32,1,4]{2,1,0:T(1,128)}), s32[32,1,4]{2,1,0:T(1,128)S(1)}, u32[]{:S(2)}, u32[]{:S(2)}) async-start(s32[32,1,4]{2,1,0:T(1,128)} %bitcast.12), calls=%async_computation.3 | async-start | bytes 32768 | tf_op jit(solution)/shard_map/all_to_all | solution.py:103
  24.9 12.9 %all-to-all-start = ((s32[32,1,64]{2,1,0:T(1,128)}), s32[32,1,64]{2,1,0:T(1,128)S(1)}, u32[]{:S(2)}, u32[]{:S(2)}) async-start(s32[32,1,64]{2,1,0:T(1,128)} %select_n.141), calls=%async_computation | async-start | bytes 32768 | tf_op jit(solution)/shard_map/all_to_all | solution.py:86
  37.8 11.9 %all-to-all-start.4 = ((bf16[32,4,768]{2,1,0:T(4,128)(2,1)}), bf16[32,4,768]{2,1,0:T(4,128)(2,1)S(1)}, u32[]{:S(2)}, u32[]{:S(2)}) async-start(bf16[32,4,768]{2,1,0:T(4,128)(2,1)} %reshape.381), calls=%async_computation.4 | async-start | bytes 393216 | tf_op jit(solution)/shard_map/all_to_all | solution.py:102
  42.9 9.9 %copy-start.7 = (s32[8]{0:T(128)S(1)}, s32[8]{0:T(128)}, u32[]{:S(2)}) copy-start(s32[8]{0:T(128)} %param.11) | copy-start | bytes 100
  49.7 73.0 %all-to-all-start.1 = ((bf16[32,64,768]{2,1,0:T(8,128)(2,1)}), bf16[32,64,768]{2,1,0:T(8,128)(2,1)S(1)}, u32[]{:S(2)}, u32[]{:S(2)}) async-start(bf16[32,64,768]{2,1,0:T(8,128)(2,1)} %bitcast.5), calls=%async_computation.1 | async-start | bytes 6291456 | tf_op jit(solution)/shard_map/all_to_all | solution.py:85
  55.4 2.5 %copy-start.4 = (s32[128]{0:T(128)}, s32[128]{0:T(128)S(1)}, u32[]{:S(2)}) copy-start(s32[128]{0:T(128)S(1)} %reshape.380) | copy-start | bytes 1540
  63.2 6.3 %copy-start.5 = (s32[128]{0:T(128)S(1)}, s32[128]{0:T(128)}, u32[]{:S(2)}) copy-start(s32[128]{0:T(128)} %copy-done.4) | copy-start | bytes 1540
  63.9 8.2 %copy-start.8 = (s32[128]{0:T(128)S(1)}, s32[128]{0:T(128)}, u32[]{:S(2)}) copy-start(s32[128]{0:T(128)} %compare_select_fusion) | copy-start | bytes 1540
  64.1 5.4 %copy-start.2 = (f32[8,768]{1,0:T(8,128)S(1)}, f32[8,768]{1,0:T(8,128)}, u32[]{:S(2)}) copy-start(f32[8,768]{1,0:T(8,128)} %param.12) | copy-start | bytes 73732
  64.1 7.0 %copy-start.3 = (f32[8,768]{1,0:T(8,128)S(1)}, f32[8,768]{1,0:T(8,128)}, u32[]{:S(2)}) copy-start(f32[8,768]{1,0:T(8,128)} %param.13) | copy-start | bytes 73732
  122.7 8.6 %copy-start.6 = (pred[8,1024]{1,0:T(8,128)(4,1)S(1)}, pred[8,1024]{1,0:T(8,128)(4,1)}, u32[]{:S(2)}) copy-start(pred[8,1024]{1,0:T(8,128)(4,1)} %iota_compare_fusion.21) | copy-start | bytes 24580
  140.4 25.5 %copy-start.1 = (s32[64,16]{1,0:T(8,128)S(1)}, s32[64,16]{1,0:T(8,128)}, u32[]{:S(2)}) copy-start(s32[64,16]{1,0:T(8,128)} %fusion.22) | copy-start | bytes 12292
  152.6 12.0 %all-to-all-start.2 = ((f32[32,1,64]{2,1,0:T(1,128)}), f32[32,1,64]{2,1,0:T(1,128)S(1)}, u32[]{:S(2)}, u32[]{:S(2)}) async-start(f32[32,1,64]{2,1,0:T(1,128)} %convolution_bitcast_fusion), calls=%async_computation.2 | async-start | bytes 32768 | tf_op jit(solution)/shard_map/all_to_all | solution.py:90
where the time goes:
time: 182 us; the launch traced here: 181 us
  waiting for transfers between devices  68.6 us (38%)
  matrix products  51 us (28%)
  other arithmetic  29.7 us (16%)
  starting transfers between devices  23.8 us (13%)
  local copies, waits for them, and re-layouts  7.32 us (4%)
    all_to_all x1, waiting for transfers between devices, local(): lax.all_to_all(sent_vectors, ('lr', 'lc'), split_axis=0, concat_axis=0, t...  49.6 us
    dot_general x1, matrix products, select_rows(): jnp.dot(onehot, table, precision=lax.Precision.HIGHEST, preferred_element...  14.7 us
    another operation x5, other arithmetic  13.5 us
    dot_general x1, matrix products, grouped_scores(): lax.dot_general(selector.astype(jnp.float32), best_flat, (((0,), (0,)), (...  12.1 us
    dot_general x1, matrix products, grouped_scores(): jnp.einsum('lkd,lrd->lkr', grouped, list_rows, preferred_element_type=jnp...  9.07 us
    dot_general x1, matrix products, grouped_scores(): jnp.dot(selector.astype(jnp.bfloat16), flat_vectors, preferred_element_ty...  8.64 us
    all_to_all x1, starting transfers between devices, local(): lax.all_to_all(new_lists, ('lr', 'lc'), split_axis=0, concat_axis=0, tile...  7.3 us
    all_to_all x1, waiting for transfers between devices, local(): lax.all_to_all(new_vectors, ('lr', 'lc'), split_axis=0, concat_axis=0, ti...  6.85 us
  transfers between devices with their start and end apart: 5, of which 4 were waited for; matrix products, arithmetic and copies ran while one was open for 22% of the time, Pallas kernels for 0%

commit v1 on v0

v1 whole, which is shorter than its diff:
```python
import functools

import jax
import jax.numpy as jnp
from jax import lax
from jax.experimental import pallas as pl
from jax.experimental.pallas import tpu as pltpu
from jax.sharding import PartitionSpec as P

AXES = ("lr", "lc")
VMEM = pl.BlockSpec(memory_space=pltpu.VMEM)
SMEM = pl.BlockSpec(memory_space=pltpu.SMEM)
BF16 = jnp.bfloat16
F32 = jnp.float32


def call(body, out_shape, *args, specs, name, scratch=(), flops=0, limit=24, alias=None):
    many = isinstance(out_shape, (list, tuple))
    return pl.pallas_call(
        body,
        in_specs=list(specs),
        out_specs=[VMEM] * len(out_shape) if many else VMEM,
        out_shape=out_shape,
        scratch_shapes=list(scratch),
        input_output_aliases=alias or {},
        compiler_params=pltpu.CompilerParams(vmem_limit_bytes=limit * 2**20),
        cost_estimate=pl.CostEstimate(flops=flops, bytes_accessed=2**20, transcendentals=0),
        name=name,
    )(*args)


def iota(shape, dim):
    return lax.broadcasted_iota(jnp.int32, shape, dim)


def mark_body(ids_ref, out_ref):
    lists = iota(out_ref.shape, 0)
    hit = lists == ids_ref[0:1, :]
    for j in range(1, ids_ref.shape[0]):
        hit = hit | (lists == ids_ref[j : j + 1, :])
    out_ref[...] = hit.astype(F32)


def rank_body(list_count, marks_ref, out_ref):
    rows, width = marks_ref.shape
    half = width // 2
    marks = marks_ref[...]
    a, b = iota((width, width), 0), iota((width, width), 1)
    same = (a // half) == (b // half)
    earlier = jnp.where(same & (a < b), 1.0, 0.0).astype(BF16)
    every = jnp.where(same, 1.0, 0.0).astype(BF16)
    r, s = iota((rows, rows), 0), iota((rows, rows), 1)
    before = jnp.where((r % list_count == s % list_count) & (s < r), 1.0, 0.0).astype(BF16)
    within = jnp.dot(marks.astype(BF16), earlier, preferred_element_type=F32)
    counts = jnp.dot(marks.astype(BF16), every, preferred_element_type=F32)
    base = jnp.dot(before, counts.astype(BF16), preferred_element_type=F32)
    out_ref[...] = jnp.where(marks > 0.5, within + base, -1.0).astype(jnp.int32)


def pair_ranks(ranks_ref, src_ref, first, list_count, half, part):
    blocks = []
    for i in range(2):
        start = pl.multiple_of(src_ref[first + i] * list_count, list_count)
        block = ranks_ref[pl.ds(start, list_count), :]
        blocks.append(block if i == part else pltpu.roll(block, half, 1))
    lane = iota(blocks[0].shape, 1)
    return jnp.where(lane < half, blocks[0], blocks[1])


def group_body(list_count, per_list, first_piece, has_in, *refs):
    src_ref, ranks_ref = refs[0], refs[1]
    refs = refs[2:]
    if has_in:
        in_ref, refs = refs[0], refs[1:]
    q_refs, out_ref, pick = refs[:-2], refs[-2], refs[-1]
    half = ranks_ref.shape[1] // 2
    depth = pick.shape[1]
    lists_a_step = pick.shape[0] // per_list
    pairs = []
    for p in range(depth // (2 * half)):
        pairs.append(pair_ranks(ranks_ref, src_ref, first_piece + 2 * p, list_count, half, 0))
    place = iota((per_list, 2 * half), 0)
    for step in range(list_count // lists_a_step):
        for i in range(lists_a_step):
            l = step * lists_a_step + i
            for p, ranks in enumerate(pairs):
                pick[i * per_list : (i + 1) * per_list, p * 2 * half : (p + 1) * 2 * half] = jnp.where(
                    ranks[l : l + 1, :] == place, 1.0, 0.0
                ).astype(BF16)
        total = None
        at = 0
        for q_ref in q_refs:
            n = q_ref.shape[0]
            term = jnp.dot(pick[:, at : at + n], q_ref[...], preferred_element_type=F32)
            total = term if total is None else total + term
            at += n
        rows = slice(step * lists_a_step * per_list, (step + 1) * lists_a_step * per_list)
        total = total.astype(BF16)
        out_ref[rows, :] = total + in_ref[rows, :] if has_in else total


def score_body(per_list, fill_ref, ranks_ref, grouped_ref, rows_ref, out_ref, best):
    list_count, row_count, _ = rows_ref.shape
    senders, _, width = out_ref.shape
    for l in range(list_count):
        scores = lax.dot_general(
            rows_ref[l],
            grouped_ref[l * per_list : (l + 1) * per_list, :],
            (((1,), (1,)), ((), ())),
            preferred_element_type=F32,
        )
        scores = jnp.where(iota(scores.shape, 0) < fill_ref[l], scores, -jnp.inf)
        best[l : l + 1, :] = jnp.max(scores, axis=0, keepdims=True)
    for s in range(senders):
        ranks = ranks_ref[s * list_count : (s + 1) * list_count, :]
        found = jnp.zeros(ranks.shape, F32)
        for c in range(per_list // width):
            index = jnp.clip(ranks - c * width, 0, width - 1)
            got = jnp.take_along_axis(best[:, c * width : (c + 1) * width], index, axis=1)
            found = jnp.where((ranks >= c * width) & (ranks < (c + 1) * width), got, found)
        out_ref[s] = found


def pick_body(got_ref, ids_ref, out_ref):
    probe_count = ids_ref.shape[0]
    lists = iota(got_ref.shape, 0)
    got = got_ref[...]
    rows = []
    for j in range(probe_count):
        rows.append(jnp.sum(jnp.where(lists == ids_ref[j : j + 1, :], got, 0.0), axis=0, keepdims=True))
    found = jnp.concatenate(rows, axis=0)
    out_ref[...] = found.T[: out_ref.shape[0], :]


def append_body(list_count, slots, src_ref, ranks_ref, center_ref, sums_ref, *refs):
    q_refs, (codes_ref, scales_ref, sums_out_ref, pick) = refs[:-4], refs[-4:]
    half = ranks_ref.shape[1] // 2
    dim = center_ref.shape[1]
    place = iota((slots, 2 * half), 0)
    piece = 0
    total = jnp.zeros((list_count * slots, dim), F32)
    live = jnp.zeros((list_count * slots, 1), F32)
    for q_ref in q_refs:
        n = q_ref.shape[0]
        for p in range(n // (2 * half)):
            ranks = pair_ranks(ranks_ref, src_ref, piece, list_count, half, 1)
            piece += 2
            for l in range(list_count):
                hit = jnp.where(ranks[l : l + 1, :] == place, 1.0, 0.0)
                pick[l * slots : (l + 1) * slots, p * 2 * half : (p + 1) * 2 * half] = hit.astype(BF16)
        chosen = pick[:, :n]
        live = live + jnp.sum(chosen.astype(F32), axis=1, keepdims=True)
        total = total + jnp.dot(chosen, q_ref[...], preferred_element_type=F32)
    for l in range(list_count):
        rows = slice(l * slots, (l + 1) * slots)
        used = live[rows, :] > 0.5
        residual = jnp.where(used, total[rows, :] - center_ref[l : l + 1, :], 0.0)
        scale = jnp.max(jnp.abs(residual), axis=1, keepdims=True) + 1e-6
        codes_ref[l] = (residual / scale).astype(BF16)
        scales_ref[l : l + 1, :] = jnp.where(used, scale, 0.0).T
        sums_out_ref[l : l + 1, :] = sums_ref[l : l + 1, :] + jnp.sum(residual, axis=0, keepdims=True)


def swap_pairs(rows, cols, of):
    pairs = []
    for lr in range(rows):
        for lc in range(cols):
            to = of(lr, lc)
            pairs.append((lr * cols + lc, to[0] * cols + to[1]))
    return pairs


def gather_queries(queries, rows, cols):
    if (rows, cols) != (8, 4):
        whole = lax.all_gather(queries, AXES, axis=0, tiled=True)
        half = whole.shape[0] // 2
        return [whole[:half], whole[half:]], jnp.arange(rows * cols, dtype=jnp.int32)

    def send(x, of):
        return lax.ppermute(x, AXES, swap_pairs(rows, cols, of))

    def plane(x):
        x = jnp.concatenate([x, send(x, lambda r, c: (r ^ (4 if r & 1 else 2), c))], 0)
        x = jnp.concatenate([x, send(x, lambda r, c: (r ^ (2 if r & 1 else 4), c))], 0)
        return [x, send(x, lambda r, c: (r ^ 1, c))]

    z = [queries] + [send(queries, lambda r, c, k=k: (r, c ^ k)) for k in (1, 2, 3)]
    chunks = plane(jnp.concatenate(z[:2], 0)) + plane(jnp.concatenate(z[2:], 0))
    r, c = lax.axis_index("lr"), lax.axis_index("lc")
    sources = []
    for base in (0, 2):
        for core in (0, 1):
            odd = (r ^ core) & 1
            one, two = jnp.where(odd == 1, 4, 2), jnp.where(odd == 1, 2, 4)
            for piece in range(8):
                row = r ^ core
                row = row ^ one if piece & 2 else row
                row = row ^ two if piece & 4 else row
                sources.append(row * cols + (c ^ (base + (piece & 1))))
    return chunks, jnp.stack(sources).astype(jnp.int32)


def local(queries, probes, assign, list_rows, list_fill, centroids, list_sums):
    rows, cols = lax.axis_size("lr"), lax.axis_size("lc")
    group = rows * cols
    list_count, row_count, dim = list_rows.shape
    query_count, probe_count = probes.shape
    pair_cap = 2 * query_count * probe_count // group
    append_cap = max(2, 2 * query_count // group)
    per_list = group * pair_cap // list_count
    slots = group * append_cap // list_count
    width = 2 * query_count
    total_lists = group * list_count

    chunks, sources = gather_queries(queries, rows, cols)

    probe_ids = probes.T
    ids = jnp.concatenate(
        [probe_ids, jnp.broadcast_to(assign[None, :], (probe_count, query_count))], axis=1
    )
    marks = call(
        mark_body,
        jax.ShapeDtypeStruct((total_lists, width), F32),
        ids,
        specs=[VMEM],
        name="mark",
    )
    marks = lax.all_to_all(
        marks.reshape(group, list_count, width), AXES, split_axis=0, concat_axis=0, tiled=True
    ).reshape(total_lists, width)
    ranks = call(
        functools.partial(rank_body, list_count),
        jax.ShapeDtypeStruct((total_lists, width), jnp.int32),
        marks,
        specs=[VMEM],
        name="rank",
    )

    grouped = None
    first = 0
    half = len(chunks) // 2
    for part in (chunks[:half], chunks[half:]):
        depth = sum(x.shape[0] for x in part)
        has_in = grouped is not None
        grouped = call(
            functools.partial(group_body, list_count, per_list, first, has_in),
            jax.ShapeDtypeStruct((list_count * per_list, dim), BF16),
            sources,
            ranks,
            *([grouped] if has_in else []),
            *part,
            specs=[SMEM] + [VMEM] * (1 + has_in + len(part)),
            scratch=[pltpu.VMEM((2 * per_list, depth), BF16)],
            flops=2 * list_count * per_list * depth * dim,
            limit=28,
            name="group",
        )
        first += depth // query_count

    best = call(
        functools.partial(score_body, per_list),
        jax.ShapeDtypeStruct((group, list_count, width), F32),
        list_fill,
        ranks,
        grouped,
        list_rows,
        specs=[SMEM, VMEM, VMEM, VMEM],
        scratch=[pltpu.VMEM((list_count, per_list), F32)],
        flops=2 * list_count * per_list * row_count * dim,
        name="score",
    )
    got = lax.all_to_all(best, AXES, split_axis=0, concat_axis=0, tiled=True)
    dup_max = call(
        pick_body,
        jax.ShapeDtypeStruct((query_count, probe_count), F32),
        got.reshape(total_lists, width),
        ids,
        specs=[VMEM, VMEM],
        name="pick",
    )

    codes, scales, new_sums = call(
        functools.partial(append_body, list_count, slots),
        [
            jax.ShapeDtypeStruct((list_count, slots, dim), BF16),
            jax.ShapeDtypeStruct((list_count, slots), F32),
            jax.ShapeDtypeStruct((list_count, dim), F32),
        ],
        sources,
        ranks,
        centroids,
        list_sums,
        *chunks,
        specs=[SMEM] + [VMEM] * (3 + len(chunks)),
        scratch=[pltpu.VMEM((list_count * slots, max(x.shape[0] for x in chunks)), BF16)],
        flops=2 * list_count * slots * group * query_count * dim,
        name="append",
    )
    return dup_max, codes, scales, new_sums


def solution(mesh):
    split = P(AXES, None)
    return jax.shard_map(
        local,
        mesh=mesh,
        in_specs=(split, split, P(AXES), P(AXES, None, None), P(AXES), split, split),
        out_specs=(split, P(AXES, None, None), split, split),
        check_vma=False,
    )
```

time: 182 us -> 72.7 us (0.40)
  matrix products: 51 us -> 0 us
  waiting for transfers between devices: 68.6 us -> 28.5 us
  other arithmetic: 29.7 us -> 1.87 us
  Pallas kernels: 0 us -> 18.1 us
  local copies, waits for them, and re-layouts: 7.32 us -> 1.9 us
  starting transfers between devices: 23.8 us -> 21.1 us
    all_to_all x5 -> x2, waiting for transfers between devices: 68.6 us -> 14.5 us  [the longest x1 8.26 us: local(): lax.all_to_all(marks.reshape(group, list_count, width), AXES, split_axis=...]
    dot_general x10 -> x0, matrix products: 51 us -> none  [the longest x1 14.7 us: select_rows(): jnp.dot(onehot, table, precision=lax.Precision.HIGHEST, preferred_element...]
    pallas_call x0 -> x7, Pallas kernels: none -> 18.1 us  [call(): pl.pallas_call(body, in_specs=list(specs), out_specs=[VMEM] * len(out_sha...]
    all_to_all x5 -> x2, starting transfers between devices: 23.8 us -> 7.98 us  [the longest x1 5.42 us: local(): lax.all_to_all(marks.reshape(group, list_count, width), AXES, split_axis=...]
    another operation x7 -> x0, other arithmetic: 14.6 us -> none
    ppermute x0 -> x9, waiting for transfers between devices: none -> 14 us  [send(): return lax.ppermute(x, AXES, swap_pairs(rows, cols, of))]
    ppermute x0 -> x9, starting transfers between devices: none -> 13.1 us  [send(): return lax.ppermute(x, AXES, swap_pairs(rows, cols, of))]
    eq x1 -> x0, other arithmetic: 4.57 us -> none  [grouped_scores(): jnp.arange(bucket_count, dtype=jnp.int32)[:, None] == bucket[None, :]]
  transfers between devices with their start and end apart: 5 -> 11, of which waited for: 4 -> 8; matrix products, arithmetic and copies ran while one was open for 22% -> 4% of each run, Pallas kernels for 0% -> 11%
where the time goes in v1:
time: 72.7 us; the launch traced here: 72.4 us
  waiting for transfers between devices  28.5 us (39%)
  starting transfers between devices  21.1 us (29%)
  Pallas kernels  18.1 us (25%)
  local copies, waits for them, and re-layouts  1.9 us (3%)
  other arithmetic  1.87 us (3%)
  between operations  0.92 us (1%)
    pallas_call x7, Pallas kernels, call(): pl.pallas_call(body, in_specs=list(specs), out_specs=[VMEM] * len(out_sha...  18.1 us
    ppermute x9, waiting for transfers between devices, send(): return lax.ppermute(x, AXES, swap_pairs(rows, cols, of))  14 us
    ppermute x9, starting transfers between devices, send(): return lax.ppermute(x, AXES, swap_pairs(rows, cols, of))  13.1 us
    all_to_all x1, waiting for transfers between devices, local(): lax.all_to_all(marks.reshape(group, list_count, width), AXES, split_axis=...  8.26 us
    all_to_all x1, waiting for transfers between devices, local(): got = lax.all_to_all(best, AXES, split_axis=0, concat_axis=0, tiled=True)  6.24 us
    all_to_all x1, starting transfers between devices, local(): lax.all_to_all(marks.reshape(group, list_count, width), AXES, split_axis=...  5.42 us
    all_to_all x1, starting transfers between devices, local(): got = lax.all_to_all(best, AXES, split_axis=0, concat_axis=0, tiled=True)  2.56 us
    unnamed x23, local copies, waits for them, and re-layouts  1.67 us
  transfers between devices with their start and end apart: 11, of which 8 were waited for; matrix products, arithmetic and copies ran while one was open for 4% of the time, Pallas kernels for 11%

profile of v1, /device:TPU:0, one launch (start us, length us, event | category | flops | bytes accessed | tf_op | source)
XLA Modules:
  0.0 72.4 jit_solution(1504924041313477701)
XLA Ops:
  0.7 3.1 %collective-permute-start = (bf16[64,768]{1,0:T(8,128)(2,1)}, bf16[64,768]{1,0:T(8,128)(2,1)S(1)}, u32[]{:S(2)}, u32[]{:S(2)}) collective-permute-start(bf16[64,768]{1,0:T(8,128)(2,1)} %param.7), channel_id=1, source_target_pairs={{0,1},{1,0},{2,3},{3,2},{4,5},{5,4},{6,7},{7,6},{8,9},{9,8},{10,11... | collective-permute-start | bytes 294920 | tf_op jit(solution)/shard_map/ppermute | solution.py:180
  3.7 2.5 %collective-permute-start.5 = (bf16[64,768]{1,0:T(8,128)(2,1)}, bf16[64,768]{1,0:T(8,128)(2,1)S(1)}, u32[]{:S(2)}, u32[]{:S(2)}) collective-permute-start(bf16[64,768]{1,0:T(8,128)(2,1)} %param.7), channel_id=1, source_target_pairs={{0,3},{1,2},{2,1},{3,0},{4,7},{5,6},{6,5},{7,4},{8,11},{9,10},{10,... | collective-permute-start | bytes 294920 | tf_op jit(solution)/shard_map/ppermute | solution.py:180
  6.2 0.1 collective-permute-start.4
  6.3 0.4 collective-permute-done
  6.7 0.9 %pad_maximum_fusion.2 = bf16[128,768]{1,0:T(8,128)(2,1)S(1)} fusion(bf16[64,768]{1,0:T(8,128)(2,1)S(1)} %collective-permute-done, bf16[64,768]{1,0:T(8,128)(2,1)} %param.7), kind=kLoop, calls=%fused_computation.2 | loop fusion | flops 393216 | bytes 393216 | tf_op jit(solution)/shard_map/concatenate | solution.py:188
  7.7 1.8 %collective-permute-start.1 = (bf16[128,768]{1,0:T(8,128)(2,1)S(1)}, bf16[128,768]{1,0:T(8,128)(2,1)S(1)}, u32[]{:S(2)}, u32[]{:S(2)}) collective-permute-start(bf16[128,768]{1,0:T(8,128)(2,1)S(1)} %pad_maximum_fusion.2), channel_id=1, source_target_pairs={{0,8},{1,9},{2,10},{3,11},{4,20},{5,21},{6,22},{7,23},{8,0},{9,1},... | collective-permute-start | bytes 589832 | tf_op jit(solution)/shard_map/ppermute | solution.py:180
  9.5 0.9 %constant_dynamic-update-slice_fusion.3 = bf16[512,768]{1,0:T(8,128)(2,1)S(1)} fusion(bf16[64,768]{1,0:T(8,128)(2,1)} %param.7), kind=kLoop, calls=%fused_computation.7 | loop fusion | bytes 196608
  10.4 1.8 %collective-permute-done.5 = bf16[64,768]{1,0:T(8,128)(2,1)S(1)} collective-permute-done((bf16[64,768]{1,0:T(8,128)(2,1)}, bf16[64,768]{1,0:T(8,128)(2,1)S(1)}, u32[]{:S(2)}, u32[]{:S(2)}) %collective-permute-start.5) | collective-permute-done | bytes 98336 | tf_op jit(solution)/shard_map/ppermute | solution.py:180
  12.1 3.3 %collective-permute-done.4 = bf16[64,768]{1,0:T(8,128)(2,1)S(1)} collective-permute-done((bf16[64,768]{1,0:T(8,128)(2,1)}, bf16[64,768]{1,0:T(8,128)(2,1)S(1)}, u32[]{:S(2)}, u32[]{:S(2)}) %collective-permute-start.4) | collective-permute-done | bytes 98336 | tf_op jit(solution)/shard_map/ppermute | solution.py:180
  15.4 1.6 %collective-permute-start.6 = (bf16[128,768]{1,0:T(8,128)(2,1)S(1)}, bf16[128,768]{1,0:T(8,128)(2,1)S(1)}, u32[]{:S(2)}, u32[]{:S(2)}) collective-permute-start(bf16[128,768]{1,0:T(8,128)(2,1)S(1)} %pad_maximum_fusion.3), channel_id=1, source_target_pairs={{0,8},{1,9},{2,10},{3,11},{4,20},{5,21},{6,22},{7,23},{8,0},{9,1},... | collective-permute-start | bytes 589832 | tf_op jit(solution)/shard_map/ppermute | solution.py:180
  17.0 0.9 %pad_maximum_fusion = bf16[256,768]{1,0:T(8,128)(2,1)S(1)} fusion(bf16[128,768]{1,0:T(8,128)(2,1)S(1)} %collective-permute-done.1, bf16[64,768]{1,0:T(8,128)(2,1)S(1)} %collective-permute-done, bf16[64,768]{1,0:T(8,128)(2,1)} %param.7), kind=kLoop, calls=%fused_computation | loop fusion | flops 1179648 | bytes 786432 | tf_op jit(solution)/shard_map/concatenate | solution.py:183
  17.9 1.6 %collective-permute-start.2 = (bf16[256,768]{1,0:T(8,128)(2,1)S(1)}, bf16[256,768]{1,0:T(8,128)(2,1)S(1)}, u32[]{:S(2)}, u32[]{:S(2)}) collective-permute-start(bf16[256,768]{1,0:T(8,128)(2,1)S(1)} %pad_maximum_fusion), channel_id=1, source_target_pairs={{0,16},{1,17},{2,18},{3,19},{4,12},{5,13},{6,14},{7,15},{8,24},{9,... | collective-permute-start | bytes 1179656 | tf_op jit(solution)/shard_map/ppermute | solution.py:180
  19.5 3.0 %collective-permute-done.6 = bf16[128,768]{1,0:T(8,128)(2,1)S(1)} collective-permute-done((bf16[128,768]{1,0:T(8,128)(2,1)S(1)}, bf16[128,768]{1,0:T(8,128)(2,1)S(1)}, u32[]{:S(2)}, u32[]{:S(2)}) %collective-permute-start.6) | collective-permute-done | bytes 196640 | tf_op jit(solution)/shard_map/ppermute | solution.py:180
  22.5 2.4 %collective-permute-start.7 = (bf16[256,768]{1,0:T(8,128)(2,1)S(1)}, bf16[256,768]{1,0:T(8,128)(2,1)S(1)}, u32[]{:S(2)}, u32[]{:S(2)}) collective-permute-start(bf16[256,768]{1,0:T(8,128)(2,1)S(1)} %pad_maximum_fusion.1), channel_id=1, source_target_pairs={{0,16},{1,17},{2,18},{3,19},{4,12},{5,13},{6,14},{7,15},{8,24},{9,... | collective-permute-start | bytes 1179656 | tf_op jit(solution)/shard_map/ppermute | solution.py:180
  24.9 0.9 %collective-permute-done.2 = bf16[256,768]{1,0:T(8,128)(2,1)S(1)} collective-permute-done((bf16[256,768]{1,0:T(8,128)(2,1)S(1)}, bf16[256,768]{1,0:T(8,128)(2,1)S(1)}, u32[]{:S(2)}, u32[]{:S(2)}) %collective-permute-start.2) | collective-permute-done | bytes 393248 | tf_op jit(solution)/shard_map/ppermute | solution.py:180
  25.8 0.1 collective-permute-start.3
  25.9 4.7 %collective-permute-done.7 = bf16[256,768]{1,0:T(8,128)(2,1)S(1)} collective-permute-done((bf16[256,768]{1,0:T(8,128)(2,1)S(1)}, bf16[256,768]{1,0:T(8,128)(2,1)S(1)}, u32[]{:S(2)}, u32[]{:S(2)}) %collective-permute-start.7) | collective-permute-done | bytes 393248 | tf_op jit(solution)/shard_map/ppermute | solution.py:180
  30.7 0.1 collective-permute-start.8
  30.8 0.1 pad.11.clone
  30.8 0.9 %mark.1 = f32[256,128]{1,0:T(8,128)} custom-call(s32[16,128]{1,0:T(8,128)S(1)} %pad_add_fusion.ids_ref), custom_call_target="tpu_custom_call" | custom-call | bytes 1048576 | tf_op jit(solution)/shard_map/mark/pallas_call | solution.py:19
  31.7 5.4 %all-to-all-start = ((f32[32,8,128]{2,1,0:T(8,128)}), f32[32,8,128]{2,1,0:T(8,128)S(1)}, u32[]{:S(2)}, u32[]{:S(2)}) async-start(f32[32,8,128]{2,1,0:T(8,128)} %bitcast.1), calls=%async_computation | async-start | bytes 262144 | tf_op jit(solution)/shard_map/all_to_all | solution.py:228
  37.2 0.1 stack.131.refs_0_.src_ref
  37.3 8.3 %all-to-all-done = f32[32,8,128]{2,1,0:T(8,128)S(1)} async-done(((f32[32,8,128]{2,1,0:T(8,128)}), f32[32,8,128]{2,1,0:T(8,128)S(1)}, u32[]{:S(2)}, u32[]{:S(2)}) %all-to-all-start) | async-done | bytes 131104 | tf_op jit(solution)/shard_map/all_to_all | solution.py:228
  45.6 0.4 rank.1.refs_1_.ranks_ref
  46.0 4.7 %group.2.refs_2_ = bf16[2048,768]{1,0:T(8,128)(2,1)S(1)} custom-call(s32[32]{0:T(128)S(1)} %stack.131.refs_0_.src_ref, s32[256,128]{1,0:T(8,128)S(1)} %rank.1.refs_1_.ranks_ref, bf16[512,768]{1,0:T(8,128)(2,1)S(1)} %constant_dynamic-update-slice_fusion.refs_2_.refs_0_, bf16[512,768]{1,0:T(8,128)(2,1)S(1)} %collective-permute-done.3.refs_3_.refs_1_), custom_call_target="tpu_custom_call" | custom-call | flops 3221225472 | bytes 1048576 | tf_op jit(solution)/shard_map/group/pallas_call | solution.py:19
  50.7 4.7 %group.3.grouped_ref = bf16[2048,768]{1,0:T(8,128)(2,1)S(1)} custom-call(s32[32]{0:T(128)S(1)} %stack.131.refs_0_.src_ref, s32[256,128]{1,0:T(8,128)S(1)} %rank.1.refs_1_.ranks_ref, bf16[2048,768]{1,0:T(8,128)(2,1)S(1)} %group.2.refs_2_, bf16[512,768]{1,0:T(8,128)(2,1)S(1)} %constant_dynamic-update-slice_fusion.4.refs_3_.refs_2_, ...), custom_call_target="tpu_custom_call" | custom-call | flops 3221225472 | bytes 1048576 | tf_op jit(solution)/shard_map/group/pallas_call | solution.py:19
  55.5 4.9 %score.1 = f32[32,8,128]{2,1,0:T(8,128)} custom-call(s32[8]{0:T(128)S(1)} %copy-done.2, s32[256,128]{1,0:T(8,128)S(1)} %rank.1.refs_1_.ranks_ref, bf16[2048,768]{1,0:T(8,128)(2,1)S(1)} %group.3.grouped_ref, bf16[8,1024,768]{2,1,0:T(8,128)(2,1)S(1)} %bitcast.37), custom_call_target="tpu_custom_call" | custom-call | flops 3221225472 | bytes 1048576 | tf_op jit(solution)/shard_map/score/pallas_call | solution.py:19
  60.4 2.6 %all-to-all-start.1 = ((f32[32,8,128]{2,1,0:T(8,128)}), f32[32,8,128]{2,1,0:T(8,128)S(1)}, u32[]{:S(2)}, u32[]{:S(2)}) async-start(f32[32,8,128]{2,1,0:T(8,128)} %score.1), calls=%async_computation.1 | async-start | bytes 262144 | tf_op jit(solution)/shard_map/all_to_all | solution.py:272
  62.9 2.1 %append.1 = (bf16[8,16,768]{2,1,0:T(8,128)(2,1)}, f32[8,16]{1,0:T(8,128)}, f32[8,768]{1,0:T(8,128)}) custom-call(s32[32]{0:T(128)S(1)} %stack.131.refs_0_.src_ref, s32[256,128]{1,0:T(8,128)S(1)} %rank.1.refs_1_.ranks_ref, f32[8,768]{1,0:T(8,128)S(1)} %copy-done, f32[8,768]{1,0:T(8,128)S(1)} %copy-done.1, ...), custom_call_target="tpu_custom_call" | custom-call | flops 402653184 | bytes 1048576 | tf_op jit(solution)/shard_map/append/pallas_call | solution.py:19
  65.1 6.2 %all-to-all-done.1 = f32[32,8,128]{2,1,0:T(8,128)S(1)} async-done(((f32[32,8,128]{2,1,0:T(8,128)}), f32[32,8,128]{2,1,0:T(8,128)S(1)}, u32[]{:S(2)}, u32[]{:S(2)}) %all-to-all-start.1) | async-done | bytes 131104 | tf_op jit(solution)/shard_map/all_to_all | solution.py:272
  71.3 0.4 pick.1
  71.7 0.7 copy.11
  (30 shorter events, 0.2 us)
Async XLA Ops:
  0.6 30.1 %copy-start.4 = (s32[64]{0:T(128)S(1)}, s32[64]{0:T(128)}, u32[]{:S(2)}) copy-start(s32[64]{0:T(128)} %param.9) | copy-start | bytes 772
  0.6 30.2 %copy-start.3 = (s32[64,16]{0,1:T(8,128)S(1)}, s32[64,16]{0,1:T(8,128)}, u32[]{:S(2)}) copy-start(s32[64,16]{0,1:T(8,128)} %param.8) | copy-start | bytes 12292
  0.7 6.1 %collective-permute-start = (bf16[64,768]{1,0:T(8,128)(2,1)}, bf16[64,768]{1,0:T(8,128)(2,1)S(1)}, u32[]{:S(2)}, u32[]{:S(2)}) collective-permute-start(bf16[64,768]{1,0:T(8,128)(2,1)} %param.7), channel_id=1, source_target_pairs={{0,1},{1,0},{2,3},{3,2},{4,5},{5,4},{6,7},{7,6},{8,9},{9,8},{10,11... | collective-permute-start | bytes 294920 | tf_op jit(solution)/shard_map/ppermute | solution.py:180
  3.7 8.4 %collective-permute-start.5 = (bf16[64,768]{1,0:T(8,128)(2,1)}, bf16[64,768]{1,0:T(8,128)(2,1)S(1)}, u32[]{:S(2)}, u32[]{:S(2)}) collective-permute-start(bf16[64,768]{1,0:T(8,128)(2,1)} %param.7), channel_id=1, source_target_pairs={{0,3},{1,2},{2,1},{3,0},{4,7},{5,6},{6,5},{7,4},{8,11},{9,10},{10,... | collective-permute-start | bytes 294920 | tf_op jit(solution)/shard_map/ppermute | solution.py:180
  6.2 9.2 %collective-permute-start.4 = (bf16[64,768]{1,0:T(8,128)(2,1)}, bf16[64,768]{1,0:T(8,128)(2,1)S(1)}, u32[]{:S(2)}, u32[]{:S(2)}) collective-permute-start(bf16[64,768]{1,0:T(8,128)(2,1)} %param.7), channel_id=1, source_target_pairs={{0,2},{1,3},{2,0},{3,1},{4,6},{5,7},{6,4},{7,5},{8,10},{9,11},{10,... | collective-permute-start | bytes 294920 | tf_op jit(solution)/shard_map/ppermute | solution.py:180
  7.7 9.3 %collective-permute-start.1 = (bf16[128,768]{1,0:T(8,128)(2,1)S(1)}, bf16[128,768]{1,0:T(8,128)(2,1)S(1)}, u32[]{:S(2)}, u32[]{:S(2)}) collective-permute-start(bf16[128,768]{1,0:T(8,128)(2,1)S(1)} %pad_maximum_fusion.2), channel_id=1, source_target_pairs={{0,8},{1,9},{2,10},{3,11},{4,20},{5,21},{6,22},{7,23},{8,0},{9,1},... | collective-permute-start | bytes 589832 | tf_op jit(solution)/shard_map/ppermute | solution.py:180
  15.4 7.1 %collective-permute-start.6 = (bf16[128,768]{1,0:T(8,128)(2,1)S(1)}, bf16[128,768]{1,0:T(8,128)(2,1)S(1)}, u32[]{:S(2)}, u32[]{:S(2)}) collective-permute-start(bf16[128,768]{1,0:T(8,128)(2,1)S(1)} %pad_maximum_fusion.3), channel_id=1, source_target_pairs={{0,8},{1,9},{2,10},{3,11},{4,20},{5,21},{6,22},{7,23},{8,0},{9,1},... | collective-permute-start | bytes 589832 | tf_op jit(solution)/shard_map/ppermute | solution.py:180
  17.9 7.8 %collective-permute-start.2 = (bf16[256,768]{1,0:T(8,128)(2,1)S(1)}, bf16[256,768]{1,0:T(8,128)(2,1)S(1)}, u32[]{:S(2)}, u32[]{:S(2)}) collective-permute-start(bf16[256,768]{1,0:T(8,128)(2,1)S(1)} %pad_maximum_fusion), channel_id=1, source_target_pairs={{0,16},{1,17},{2,18},{3,19},{4,12},{5,13},{6,14},{7,15},{8,24},{9,... | collective-permute-start | bytes 1179656 | tf_op jit(solution)/shard_map/ppermute | solution.py:180
  22.5 8.1 %collective-permute-start.7 = (bf16[256,768]{1,0:T(8,128)(2,1)S(1)}, bf16[256,768]{1,0:T(8,128)(2,1)S(1)}, u32[]{:S(2)}, u32[]{:S(2)}) collective-permute-start(bf16[256,768]{1,0:T(8,128)(2,1)S(1)} %pad_maximum_fusion.1), channel_id=1, source_target_pairs={{0,16},{1,17},{2,18},{3,19},{4,12},{5,13},{6,14},{7,15},{8,24},{9,... | collective-permute-start | bytes 1179656 | tf_op jit(solution)/shard_map/ppermute | solution.py:180
  25.8 20.2 %collective-permute-start.3 = (bf16[512,768]{1,0:T(8,128)(2,1)S(1)}, bf16[512,768]{1,0:T(8,128)(2,1)S(1)}, u32[]{:S(2)}, u32[]{:S(2)}) collective-permute-start(bf16[512,768]{1,0:T(8,128)(2,1)S(1)} %constant_dynamic-update-slice_fusion.refs_2_.refs_0_), channel_id=1, source_target_pairs={{0,4},{1,5},{2,6},{3,7},{4,0},{5,1},{6,2},{7,3},{8,12},{9,13},{10,... | collective-permute-start | bytes 2359304 | tf_op jit(solution)/shard_map/ppermute | solution.py:180
  30.7 20.0 %collective-permute-start.8 = (bf16[512,768]{1,0:T(8,128)(2,1)S(1)}, bf16[512,768]{1,0:T(8,128)(2,1)S(1)}, u32[]{:S(2)}, u32[]{:S(2)}) collective-permute-start(bf16[512,768]{1,0:T(8,128)(2,1)S(1)} %constant_dynamic-update-slice_fusion.4.refs_3_.refs_2_), channel_id=1, source_target_pairs={{0,4},{1,5},{2,6},{3,7},{4,0},{5,1},{6,2},{7,3},{8,12},{9,13},{10,... | collective-permute-start | bytes 2359304 | tf_op jit(solution)/shard_map/ppermute | solution.py:180
  31.7 13.8 %all-to-all-start = ((f32[32,8,128]{2,1,0:T(8,128)}), f32[32,8,128]{2,1,0:T(8,128)S(1)}, u32[]{:S(2)}, u32[]{:S(2)}) async-start(f32[32,8,128]{2,1,0:T(8,128)} %bitcast.1), calls=%async_computation | async-start | bytes 262144 | tf_op jit(solution)/shard_map/all_to_all | solution.py:228
  46.0 9.4 %slice-start = ((s8[12582912]{0:T(1024)(128)(4,1)}), s8[4194304]{0:T(1024)(128)(4,1)S(1)}, s32[]{:S(2)}) async-start(s8[12582912]{0:T(1024)(128)(4,1)} %bitcast.36), calls=%async_computation.2 | async-start | bytes 8388608
  46.0 9.4 %slice-start.1 = ((s8[12582912]{0:T(1024)(128)(4,1)}), s8[4194304]{0:T(1024)(128)(4,1)S(1)}, s32[]{:S(2)}) async-start(s8[12582912]{0:T(1024)(128)(4,1)} %bitcast.36), calls=%async_computation.3 | async-start | bytes 8388608
  50.7 4.8 %slice-start.2 = ((s8[12582912]{0:T(1024)(128)(4,1)}), s8[4194304]{0:T(1024)(128)(4,1)S(1)}, s32[]{:S(2)}) async-start(s8[12582912]{0:T(1024)(128)(4,1)} %bitcast.36), calls=%async_computation.4 | async-start | bytes 8388608
  50.7 4.8 %copy-start.2 = (s32[8]{0:T(128)S(1)}, s32[8]{0:T(128)}, u32[]{:S(2)}) copy-start(s32[8]{0:T(128)} %fill_ref.1) | copy-start | bytes 100
  55.4 7.5 %copy-start = (f32[8,768]{1,0:T(8,128)S(1)}, f32[8,768]{1,0:T(8,128)}, u32[]{:S(2)}) copy-start(f32[8,768]{1,0:T(8,128)} %center_ref.1) | copy-start | bytes 73732
  55.5 7.5 %copy-start.1 = (f32[8,768]{1,0:T(8,128)S(1)}, f32[8,768]{1,0:T(8,128)}, u32[]{:S(2)}) copy-start(f32[8,768]{1,0:T(8,128)} %sums_ref.1) | copy-start | bytes 73732
  60.4 11.0 %all-to-all-start.1 = ((f32[32,8,128]{2,1,0:T(8,128)}), f32[32,8,128]{2,1,0:T(8,128)S(1)}, u32[]{:S(2)}, u32[]{:S(2)}) async-start(f32[32,8,128]{2,1,0:T(8,128)} %score.1), calls=%async_computation.1 | async-start | bytes 262144 | tf_op jit(solution)/shard_map/all_to_all | solution.py:272
